TPU v7x, 32 devices: a whole 2x2x4 slice. The times are simulated.
32 devices in a mesh: groups: 2 (over y), context: 4 (over z), tensor: 4 (over x, core).
Axes of the slice: x: 2, y: 2, z: 4, core: 2. Of those that a mesh axis runs over, the one named last changes fastest.
Arguments:
- inputs: bfloat16 [4096, 1024], P(('groups', 'context')), parts along dimension 0, may hold values from -6 to 6
- frame_valid: int32 [4096], P(('groups', 'context')), parts along dimension 0, may hold values from 0 to 1, as said below
- norm1_gain: float32 [1024], replicated, may hold values from 0.1 to 1.9
- w_query: bfloat16 [1024, 1024], P(None, 'tensor')
- w_key: bfloat16 [1024, 1024], P(None, 'tensor')
- w_value: bfloat16 [1024, 1024], P(None, 'tensor'), may hold values from -0.1875 to 0.1875
- w_out: bfloat16 [1024, 1024], P('tensor'), may hold values from -0.1875 to 0.1875
- norm2_gain: float32 [1024], replicated, may hold values from 0.1 to 1.9
- w_point1: bfloat16 [2, 1024, 1024], P(None, None, 'tensor'), may hold values from -0.1875 to 0.1875
- w_depth: float32 [31, 1024], P(None, 'tensor'), may hold values from -1.5 to 1.5
- bn_scale: float32 [1024], P('tensor'), may hold values from 0.1 to 1.9
- bn_shift: float32 [1024], P('tensor'), may hold values from -1 to 1
- w_point2: bfloat16 [1024, 1024], P('tensor'), may hold values from -0.1875 to 0.1875
Outputs:
- output: bfloat16 [4096, 1024], P(('groups', 'context', 'tensor')), parts along dimension 0
There are 2 independent parts, one for each index of `groups`. A program takes and returns all parts, laid end to end along the dimension named above; an argument that names none is the same for every part. Nothing has to cross between parts.
Inputs may be any that keep to these rules, and one draw needn't show every extreme that they name: `frame_valid`: the transcript frames form a prefix of the window of at least 1024 frames, followed by at least one padded frame.
All inputs are finite; a program needn't handle non-finite values.
Results may differ from a plain program's by a relative error of at most 0.0095.
Values may be sent and summed in bfloat16 or wider, within the bound.
A program may use at most 64 MiB of HBM per device.

v0:
```python
import math

import jax
import jax.numpy as jnp
from jax import lax
from jax.sharding import PartitionSpec as P

HD = 64


NEG = -1e30


def with_halo(block, sides, width):
    for axis, dim in sides:
        count = lax.axis_size(axis)
        forward = [(i, i + 1) for i in range(count - 1)]
        backward = [(target, source) for source, target in forward]
        low = lax.ppermute(
            lax.slice_in_dim(block, block.shape[dim] - width, None, axis=dim), axis, forward
        )
        high = lax.ppermute(lax.slice_in_dim(block, 0, width, axis=dim), axis, backward)
        block = jnp.concatenate([low, block, high], axis=dim)
    return block


def normalize(rows, gain):
    values = rows.astype(jnp.float32)
    center = jnp.mean(values, axis=-1, keepdims=True)
    spread = jnp.mean(jnp.square(values - center), axis=-1, keepdims=True)
    return ((values - center) * lax.rsqrt(spread + 1e-05) * gain).astype(jnp.bfloat16)


def local(
    inputs,
    frame_valid,
    norm1_gain,
    w_query,
    w_key,
    w_value,
    w_out,
    norm2_gain,
    w_point1,
    w_depth,
    bn_scale,
    bn_shift,
    w_point2,
):
    frames = inputs.shape[0]
    local_cols = w_query.shape[1]
    head_dim = HD
    heads_here = local_cols // head_dim
    scale = 1.0 / math.sqrt(head_dim)
    normed = normalize(inputs, norm1_gain)
    query = jnp.dot(normed, w_query, preferred_element_type=jnp.float32).astype(jnp.bfloat16)
    query = query.reshape(frames, heads_here, head_dim)
    keys = jnp.dot(normed, w_key, preferred_element_type=jnp.float32).astype(jnp.bfloat16)
    vals = jnp.dot(normed, w_value, preferred_element_type=jnp.float32).astype(jnp.bfloat16)

    def update(carry, key_blk, val_blk, valid_blk):
        run_max, run_sum, accum = carry
        rows = key_blk.shape[0]
        key_heads = key_blk.reshape(rows, heads_here, head_dim)
        val_heads = val_blk.reshape(rows, heads_here, head_dim)
        scores = (
            jnp.einsum("qhd,khd->hqk", query, key_heads, preferred_element_type=jnp.float32) * scale
        )
        live = (valid_blk > 0)[None, None, :]
        scores = jnp.where(live, scores, NEG)
        new_max = jnp.maximum(run_max, jnp.max(scores, axis=-1))
        weights = jnp.where(live, jnp.exp(scores - new_max[:, :, None]), 0.0)
        factor = jnp.exp(run_max - new_max)
        run_sum = run_sum * factor + jnp.sum(weights, axis=-1)
        mixed = jnp.einsum(
            "hqk,khd->qhd",
            weights.astype(jnp.bfloat16),
            val_heads,
            preferred_element_type=jnp.float32,
        )
        accum = accum * jnp.repeat(factor.T, head_dim, axis=1) + mixed.reshape(frames, local_cols)
        return (new_max, run_sum, accum)

    def visit(carry, key_blk, val_blk, valid_blk):
        return update(carry, key_blk, val_blk, valid_blk)

    start_state = (
        jnp.full((heads_here, frames), NEG, jnp.float32),
        jnp.zeros((heads_here, frames), jnp.float32),
        jnp.zeros((frames, local_cols), jnp.float32),
    )
    carry = start_state
    key_part = lax.all_gather(keys, "context", axis=0, tiled=True)
    val_part = lax.all_gather(vals, "context", axis=0, tiled=True)
    valid_part = lax.all_gather(frame_valid, "context", axis=0, tiled=True)
    rows = key_part.shape[0]
    shards = max(rows // frames, 1)
    group = math.gcd(shards, max(1536 // frames, 1))
    blocks = shards // group
    block_rows = rows // blocks

    def advance(state, items):
        return (visit(state, items[0], items[1], items[2]), None)

    stacked = (
        key_part.reshape(blocks, block_rows, local_cols),
        val_part.reshape(blocks, block_rows, local_cols),
        valid_part.reshape(blocks, block_rows),
    )
    carry, unused = lax.scan(advance, carry, stacked)
    run_max, run_sum, accum = carry
    attended = (accum / jnp.repeat(run_sum.T, head_dim, axis=1)).astype(jnp.bfloat16)
    share = frames // lax.axis_size("tensor")
    first_row = lax.axis_index("tensor") * share
    total = lax.psum(jnp.dot(attended, w_out, preferred_element_type=jnp.float32), "tensor")
    residual = (inputs.astype(jnp.float32) + total).astype(jnp.bfloat16)
    normed_two = normalize(residual, norm2_gain)
    residual_rows = lax.dynamic_slice_in_dim(residual, first_row, share, 0)
    value_half = jnp.dot(normed_two, w_point1[0], preferred_element_type=jnp.float32)
    gate_half = jnp.dot(normed_two, w_point1[1], preferred_element_type=jnp.float32)
    gated = jnp.where(
        (frame_valid > 0)[:, None], value_half * jax.nn.sigmoid(gate_half), 0.0
    ).astype(jnp.bfloat16)
    taps = w_depth.shape[0]
    half = (taps - 1) // 2
    padded = with_halo(gated, (("context", 0),), half)
    depth = jnp.zeros((frames, gated.shape[1]), jnp.float32)
    for tap in range(taps):
        depth = depth + padded[tap : tap + frames].astype(jnp.float32) * w_depth[tap]
    activated = jax.nn.silu(depth * bn_scale + bn_shift).astype(jnp.bfloat16)
    conv_rows = lax.psum_scatter(
        jnp.dot(activated, w_point2, preferred_element_type=jnp.float32).astype(jnp.bfloat16),
        "tensor",
        scatter_dimension=0,
        tiled=True,
    ).astype(jnp.float32)
    return (residual_rows.astype(jnp.float32) + conv_rows).astype(jnp.bfloat16)


def solution(mesh):
    placed = (
        P(("groups", "context"), None),
        P(("groups", "context")),
        P(),
        P(None, "tensor"),
        P(None, "tensor"),
        P(None, "tensor"),
        P("tensor", None),
        P(),
        P(None, None, "tensor"),
        P(None, "tensor"),
        P("tensor"),
        P("tensor"),
        P("tensor", None),
    )
    return jax.shard_map(
        local,
        mesh=mesh,
        in_specs=placed,
        out_specs=P(("groups", "context", "tensor"), None),
        check_vma=False,
    )
```

profile of v0, /device:TPU:11, one launch (start us, length us, event | category | flops | bytes accessed | tf_op | source)
XLA Modules:
  0.0 215.7 jit_solution(7202695658550756041)
XLA Ops:
  6.6 1.6 convert_reduce_fusion
  8.2 1.6 fusion.17
  9.9 1.2 convolution_convert_fusion.3
  11.2 1.2 convolution_convert_fusion.1
  12.5 9.5 %all-gather = s32[4,1,512]{2,1,0:T(1,128)S(1)} all-gather(s32[1,1,512]{2,1,0:T(1,128)S(1)} %bitcast.111), channel_id=1, replica_groups=mesh['groups'=2,'context'=4,'tensor'=4] {'context'}, dimensions={0}, use_global_device_ids=true | all-gather | bytes 10240 | tf_op jit(solution)/shard_map/all_gather | solution.py:94
  22.0 1.7 convolution_convert_fusion.2
  23.8 16.3 %all-gather.4.cloned.1.call-done = bf16[2048,256]{1,0:T(8,128)(2,1)} async-done(((bf16[512,256]{1,0:T(8,128)(2,1)}), bf16[2048,256]{1,0:T(8,128)(2,1)}) %all-gather.4.cloned.1.call-update) | async-done | bytes 1048592 | tf_op jit(solution)/shard_map/all_gather | solution.py:92
  40.1 29.0 %all-gather.6.cloned.1.call-done = bf16[2048,256]{1,0:T(8,128)(2,1)} async-done(((bf16[512,256]{1,0:T(8,128)(2,1)}), bf16[2048,256]{1,0:T(8,128)(2,1)}) %all-gather.6.cloned.1.call-update) | async-done | bytes 1048592 | tf_op jit(solution)/shard_map/all_gather | solution.py:93
  69.1 44.4 %while.15 = (s32[]{:T(128)}, f32[4,512]{1,0:T(4,128)S(1)}, f32[4,512]{1,0:T(4,128)S(1)}, f32[512,256]{0,1:T(8,128)S(1)}, s32[4,512]{1,0:T(4,128)S(1)}, /*index=5...) while((s32[]{:T(128)}, f32[4,512]{1,0:T(4,128)S(1)}, ...), condition=%wide.region_5.6_spmd.clone, body=%wide.region_2.5_spmd.clone.sunk | while | flops 282472960 | bytes 17698944 | solution.py:109
  69.1 1.1 constant_dynamic-slice_fusion.3
  70.2 0.1 copy.28
  70.4 2.9 %bitcast_reduce_fusion.2 = (f32[4,512]{1,0:T(4,128)S(1)}, f32[4,512,512]{2,1,0:T(8,128)}) fusion(pred[512]{0:T(512)(128)(4,1)S(1)} %compare_reduce_fusion.2, bf16[512,4,64]{0,2,1:T(8,128)(2,1)S(1)} %bitcast.104, bf16[512,4,64]{0,2,1:T(8,128)(2,1)S(1)} %get-tuple-element.237), kind=kOutput, calls=%fused_computation.1.clone.1 | convolution fusion | flops 137361408 | bytes 4727296 | tf_op jit(solution)/shard_map/while/body/eval_jaxpr/qhd,khd->hqk/dot_general | solution.py:66
  73.3 3.3 %fusion.96 = f32[4,512]{1,0:T(4,128)S(1)} fusion(f32[4,512,512]{2,1,0:T(8,128)} %get-tuple-element.208, f32[4,512]{1,0:T(4,128)S(1)} %get-tuple-element.232, pred[512]{0:T(512)(128)(4,1)S(1)} %compare_reduce_fusion.2), kind=kLoop, calls=%fused_computation.6.clone.1 | loop fusion | flops 5240832 | bytes 4211200 | tf_op jit(solution)/shard_map/while/body/eval_jaxpr/reduce_sum | solution.py:73
  76.6 0.1 copy.29
  76.7 3.3 %fusion.98 = f32[4,64,512]{2,1,0:T(8,128)S(1)} fusion(bf16[512,4,64]{0,2,1:T(8,128)(2,1)S(1)} %bitcast.106, f32[4,512,512]{2,1,0:T(8,128)} %get-tuple-element.208, f32[4,512]{1,0:T(4,128)S(1)} %get-tuple-element.232, pred[512]{0:T(512)(128)(4,1)S(1)} %compare_reduce_fusion.2), kind=kOutput, calls=%fused_computation.7.clone.1 | convolution fusion | flops 139460608 | bytes 4989440 | tf_op jit(solution)/shard_map/while/body/eval_jaxpr/hqk,khd->qhd/dot_general | solution.py:74
  80.0 0.2 bitcast_add_fusion.2
  80.2 1.1 constant_dynamic-slice_fusion.3
  81.3 0.1 copy.28
  81.5 2.9 %bitcast_reduce_fusion.2 = (f32[4,512]{1,0:T(4,128)S(1)}, f32[4,512,512]{2,1,0:T(8,128)}) fusion(pred[512]{0:T(512)(128)(4,1)S(1)} %compare_reduce_fusion.2, bf16[512,4,64]{0,2,1:T(8,128)(2,1)S(1)} %bitcast.104, bf16[512,4,64]{0,2,1:T(8,128)(2,1)S(1)} %get-tuple-element.237), kind=kOutput, calls=%fused_computation.1.clone.1 | convolution fusion | flops 137361408 | bytes 4727296 | tf_op jit(solution)/shard_map/while/body/eval_jaxpr/qhd,khd->hqk/dot_general | solution.py:66
  84.4 3.3 %fusion.96 = f32[4,512]{1,0:T(4,128)S(1)} fusion(f32[4,512,512]{2,1,0:T(8,128)} %get-tuple-element.208, f32[4,512]{1,0:T(4,128)S(1)} %get-tuple-element.232, pred[512]{0:T(512)(128)(4,1)S(1)} %compare_reduce_fusion.2), kind=kLoop, calls=%fused_computation.6.clone.1 | loop fusion | flops 5240832 | bytes 4211200 | tf_op jit(solution)/shard_map/while/body/eval_jaxpr/reduce_sum | solution.py:73
  87.7 0.1 copy.29
  87.8 3.3 %fusion.98 = f32[4,64,512]{2,1,0:T(8,128)S(1)} fusion(bf16[512,4,64]{0,2,1:T(8,128)(2,1)S(1)} %bitcast.106, f32[4,512,512]{2,1,0:T(8,128)} %get-tuple-element.208, f32[4,512]{1,0:T(4,128)S(1)} %get-tuple-element.232, pred[512]{0:T(512)(128)(4,1)S(1)} %compare_reduce_fusion.2), kind=kOutput, calls=%fused_computation.7.clone.1 | convolution fusion | flops 139460608 | bytes 4989440 | tf_op jit(solution)/shard_map/while/body/eval_jaxpr/hqk,khd->qhd/dot_general | solution.py:74
  91.1 0.2 bitcast_add_fusion.2
  91.4 1.1 constant_dynamic-slice_fusion.3
  92.4 0.1 copy.28
  92.6 2.9 %bitcast_reduce_fusion.2 = (f32[4,512]{1,0:T(4,128)S(1)}, f32[4,512,512]{2,1,0:T(8,128)}) fusion(pred[512]{0:T(512)(128)(4,1)S(1)} %compare_reduce_fusion.2, bf16[512,4,64]{0,2,1:T(8,128)(2,1)S(1)} %bitcast.104, bf16[512,4,64]{0,2,1:T(8,128)(2,1)S(1)} %get-tuple-element.237), kind=kOutput, calls=%fused_computation.1.clone.1 | convolution fusion | flops 137361408 | bytes 4727296 | tf_op jit(solution)/shard_map/while/body/eval_jaxpr/qhd,khd->hqk/dot_general | solution.py:66
  95.5 3.3 %fusion.96 = f32[4,512]{1,0:T(4,128)S(1)} fusion(f32[4,512,512]{2,1,0:T(8,128)} %get-tuple-element.208, f32[4,512]{1,0:T(4,128)S(1)} %get-tuple-element.232, pred[512]{0:T(512)(128)(4,1)S(1)} %compare_reduce_fusion.2), kind=kLoop, calls=%fused_computation.6.clone.1 | loop fusion | flops 5240832 | bytes 4211200 | tf_op jit(solution)/shard_map/while/body/eval_jaxpr/reduce_sum | solution.py:73
  98.8 0.1 copy.29
  99.0 3.3 %fusion.98 = f32[4,64,512]{2,1,0:T(8,128)S(1)} fusion(bf16[512,4,64]{0,2,1:T(8,128)(2,1)S(1)} %bitcast.106, f32[4,512,512]{2,1,0:T(8,128)} %get-tuple-element.208, f32[4,512]{1,0:T(4,128)S(1)} %get-tuple-element.232, pred[512]{0:T(512)(128)(4,1)S(1)} %compare_reduce_fusion.2), kind=kOutput, calls=%fused_computation.7.clone.1 | convolution fusion | flops 139460608 | bytes 4989440 | tf_op jit(solution)/shard_map/while/body/eval_jaxpr/hqk,khd->qhd/dot_general | solution.py:74
  102.2 0.2 bitcast_add_fusion.2
  102.5 1.1 constant_dynamic-slice_fusion.3
  103.5 0.1 copy.28
  103.7 2.9 %bitcast_reduce_fusion.2 = (f32[4,512]{1,0:T(4,128)S(1)}, f32[4,512,512]{2,1,0:T(8,128)}) fusion(pred[512]{0:T(512)(128)(4,1)S(1)} %compare_reduce_fusion.2, bf16[512,4,64]{0,2,1:T(8,128)(2,1)S(1)} %bitcast.104, bf16[512,4,64]{0,2,1:T(8,128)(2,1)S(1)} %get-tuple-element.237), kind=kOutput, calls=%fused_computation.1.clone.1 | convolution fusion | flops 137361408 | bytes 4727296 | tf_op jit(solution)/shard_map/while/body/eval_jaxpr/qhd,khd->hqk/dot_general | solution.py:66
  106.6 3.3 %fusion.96 = f32[4,512]{1,0:T(4,128)S(1)} fusion(f32[4,512,512]{2,1,0:T(8,128)} %get-tuple-element.208, f32[4,512]{1,0:T(4,128)S(1)} %get-tuple-element.232, pred[512]{0:T(512)(128)(4,1)S(1)} %compare_reduce_fusion.2), kind=kLoop, calls=%fused_computation.6.clone.1 | loop fusion | flops 5240832 | bytes 4211200 | tf_op jit(solution)/shard_map/while/body/eval_jaxpr/reduce_sum | solution.py:73
  110.1 3.3 %fusion.98 = f32[4,64,512]{2,1,0:T(8,128)S(1)} fusion(bf16[512,4,64]{0,2,1:T(8,128)(2,1)S(1)} %bitcast.106, f32[4,512,512]{2,1,0:T(8,128)} %get-tuple-element.208, f32[4,512]{1,0:T(4,128)S(1)} %get-tuple-element.232, pred[512]{0:T(512)(128)(4,1)S(1)} %compare_reduce_fusion.2), kind=kOutput, calls=%fused_computation.7.clone.1 | convolution fusion | flops 139460608 | bytes 4989440 | tf_op jit(solution)/shard_map/while/body/eval_jaxpr/hqk,khd->qhd/dot_general | solution.py:74
  113.3 0.2 bitcast_add_fusion.2
  113.6 1.8 fusion.73
  115.5 50.4 %all-reduce.2.cloned.1.call-done = f32[512,1024]{1,0:T(8,128)} async-done(((f32[512,1024]{1,0:T(8,128)}), f32[512,1024]{1,0:T(8,128)}) %all-reduce.2.cloned.1.call-update) | async-done | bytes 2097168 | tf_op jit(solution)/shard_map/psum | solution.py:114
  166.0 2.0 convert_reduce_fusion.1
  168.0 0.4 fusion.20
  168.4 0.5 fusion.27
  169.0 0.5 fusion.28
  169.5 2.1 collective-permute-start.1
  171.6 3.2 %collective-permute-start = (bf16[15,256]{1,0:T(8,128)(2,1)S(1)}, bf16[15,256]{1,0:T(8,128)(2,1)S(1)}, u32[]{:S(2)}, u32[]{:S(2)}) collective-permute-start(bf16[15,256]{1,0:T(8,128)(2,1)S(1)} %get-tuple-element.117), channel_id=1, source_target_pairs={{0,4},{4,8},{8,12},{1,5},{5,9},{9,13},{2,6},{6,10},{10,14},{3,7},{... | collective-permute-start | bytes 23048 | tf_op jit(solution)/shard_map/ppermute | solution.py:19
  174.9 1.1 collective-permute-done
  176.0 4.9 %convolution_convert_fusion = bf16[512,1024]{1,0:T(8,128)(2,1)} fusion(bf16[256,1024]{1,0:T(8,128)(2,1)S(1)} %copy-done.7, bf16[512,256]{1,0:T(8,128)(2,1)S(1)} %fusion.28, bf16[15,256]{1,0:T(8,128)(2,1)S(1)} %collective-permute-done.1, bf16[15,256]{1,0:T(8,128)(2,1)S(1)} %collective-permute-done, f32[256]{0:T(256)S(1)} %copy-done.10, ...), kind=kOutput, calls=%fused_computation.67 | convolution fusion | flops 293732352 | bytes 1884160 | tf_op jit(solution)/shard_map/dot_general | solution.py:131
  181.0 26.5 %reduce-scatter.2.cloned.1.call-done = bf16[128,1024]{1,0:T(8,128)(2,1)} async-done(((bf16[512,1024]{1,0:T(8,128)(2,1)}), bf16[128,1024]{1,0:T(8,128)(2,1)}) %reduce-scatter.2.cloned.1.call-update) | async-done | bytes 262160 | tf_op jit(solution)/shard_map/reduce_scatter | solution.py:130
  207.5 1.7 add_convert_fusion
  (63 shorter events, 0.8 us)
Async XLA Ops:
  6.5 107.1 %copy-start = (bf16[256,1024]{1,0:T(8,128)(2,1)S(1)}, bf16[256,1024]{1,0:T(8,128)(2,1)}, u32[]{:S(2)}) copy-start(bf16[256,1024]{1,0:T(8,128)(2,1)} %param.21) | copy-start | bytes 1572868
  6.5 3.3 %copy-start.1 = (bf16[512,1024]{1,0:T(8,128)(2,1)S(1)}, bf16[512,1024]{1,0:T(8,128)(2,1)}, u32[]{:S(2)}) copy-start(bf16[512,1024]{1,0:T(8,128)(2,1)} %param.15) | copy-start | bytes 3145732
  6.5 3.3 %copy-start.5 = (bf16[1024,256]{1,0:T(8,128)(2,1)S(1)}, bf16[1024,256]{1,0:T(8,128)(2,1)}, u32[]{:S(2)}) copy-start(bf16[1024,256]{1,0:T(8,128)(2,1)} %param.19) | copy-start | bytes 1572868
  6.5 3.3 %copy-start.8 = (f32[1024]{0:T(1024)S(1)}, f32[1024]{0:T(1024)}, u32[]{:S(2)}) copy-start(f32[1024]{0:T(1024)} %param.17) | copy-start | bytes 12292
  6.5 33.5 %all-gather.4.cloned.1.call-start = ((), (), s32[]{:S(2)}) async-start(), calls=%async_computation.1 | async-start | bytes 1310720 | tf_op jit(solution)/shard_map/all_gather | solution.py:92
  9.8 1.4 copy-start.6
  11.1 1.4 copy-start.3
  11.1 58.0 %all-gather.6.cloned.1.call-start = ((), (), s32[]{:S(2)}) async-start(), calls=%async_computation.2 | async-start | bytes 1310720 | tf_op jit(solution)/shard_map/all_gather | solution.py:93
  12.4 153.5 %all-reduce.2.cloned.1.call-start = ((), (), s32[]{:S(2)}) async-start(), calls=%async_computation.3 | async-start | bytes 4194304 | tf_op jit(solution)/shard_map/psum | solution.py:114
  113.6 1.9 copy-start.2
  115.4 92.0 %reduce-scatter.2.cloned.1.call-start = ((), (), s32[]{:S(2)}) async-start(), calls=%async_computation.4 | async-start | bytes 1310720 | tf_op jit(solution)/shard_map/reduce_scatter | solution.py:130
  115.5 52.9 %copy-start.9 = (f32[1024]{0:T(1024)S(1)}, f32[1024]{0:T(1024)}, u32[]{:S(2)}) copy-start(f32[1024]{0:T(1024)} %param.22) | copy-start | bytes 12292
  166.0 2.4 %copy-start.4 = (bf16[2,1024,256]{2,1,0:T(8,128)(2,1)S(1)}, bf16[2,1024,256]{2,1,0:T(8,128)(2,1)}, u32[]{:S(2)}) copy-start(bf16[2,1024,256]{2,1,0:T(8,128)(2,1)} %param.23) | copy-start | bytes 3145732
  169.0 7.1 %copy-start.7 = (bf16[256,1024]{1,0:T(8,128)(2,1)S(1)}, bf16[256,1024]{1,0:T(8,128)(2,1)}, u32[]{:S(2)}) copy-start(bf16[256,1024]{1,0:T(8,128)(2,1)} %param.27) | copy-start | bytes 1572868
  169.0 7.1 %copy-start.10 = (f32[256]{0:T(256)S(1)}, f32[256]{0:T(256)}, u32[]{:S(2)}) copy-start(f32[256]{0:T(256)} %param.26) | copy-start | bytes 3076
  169.0 7.0 %copy-start.11 = (f32[256]{0:T(256)S(1)}, f32[256]{0:T(256)}, u32[]{:S(2)}) copy-start(f32[256]{0:T(256)} %param.25) | copy-start | bytes 3076
  169.5 5.3 %collective-permute-start.1 = (bf16[15,256]{1,0:T(8,128)(2,1)S(1)}, bf16[15,256]{1,0:T(8,128)(2,1)S(1)}, u32[]{:S(2)}, u32[]{:S(2)}) collective-permute-start(bf16[15,256]{1,0:T(8,128)(2,1)S(1)} %get-tuple-element.118), channel_id=1, source_target_pairs={{4,0},{8,4},{12,8},{5,1},{9,5},{13,9},{6,2},{10,6},{14,10},{7,3},{... | collective-permute-start | bytes 23048 | tf_op jit(solution)/shard_map/ppermute | solution.py:22
  171.6 4.4 %collective-permute-start = (bf16[15,256]{1,0:T(8,128)(2,1)S(1)}, bf16[15,256]{1,0:T(8,128)(2,1)S(1)}, u32[]{:S(2)}, u32[]{:S(2)}) collective-permute-start(bf16[15,256]{1,0:T(8,128)(2,1)S(1)} %get-tuple-element.117), channel_id=1, source_target_pairs={{0,4},{4,8},{8,12},{1,5},{5,9},{9,13},{2,6},{6,10},{10,14},{3,7},{... | collective-permute-start | bytes 23048 | tf_op jit(solution)/shard_map/ppermute | solution.py:19
Sparse Core Ops, SparseCore 0:
  11.2 28.8 all-gather.3
  41.7 27.4 all-gather.5
  115.5 50.3 all-reduce.1
  181.1 26.3 reduce-scatter.1
where the time goes:
time: 219 us; the launch traced here: 216 us
  waiting for transfers between devices  123 us (56%)
  matrix products  36.7 us (17%)
  other arithmetic  21.4 us (10%)
  between operations  13.4 us (6%)
  blocking collectives  9.51 us (4%)
  local copies, waits for them, and re-layouts  5.5 us (3%)
  starting transfers between devices  5.44 us (2%)
    psum x1, waiting for transfers between devices, local(): lax.psum(jnp.dot(attended, w_out, preferred_element_type=jnp.float32), 't...  50.4 us
    all_gather x1, waiting for transfers between devices, local(): val_part = lax.all_gather(vals, 'context', axis=0, tiled=True)  29 us
    reduce_scatter x1, waiting for transfers between devices, local(): lax.psum_scatter(jnp.dot(activated, w_point2, preferred_element_type=jnp....  26.5 us
    all_gather x1, waiting for transfers between devices, local(): key_part = lax.all_gather(keys, 'context', axis=0, tiled=True)  16.3 us
    dot_general x4, matrix products, update(): jnp.einsum('hqk,khd->qhd', weights.astype(jnp.bfloat16), val_heads, prefe...  13.1 us
    reduce_sum x4, other arithmetic, update(): run_sum = run_sum * factor + jnp.sum(weights, axis=-1)  13.1 us
    dot_general x4, matrix products, update(): jnp.einsum('qhd,khd->hqk', query, key_heads, preferred_element_type=jnp.f...  11.6 us
    all_gather x1, blocking collectives, local(): valid_part = lax.all_gather(frame_valid, 'context', axis=0, tiled=True)  9.51 us
  transfers between devices with their start and end apart: 6, of which 5 were waited for; matrix products, arithmetic and copies ran while one was open for 1% of the time, Pallas kernels for 0%

commit v1 on v0

v1 whole, which is shorter than its diff:
```python
import functools
import math

import jax
import jax.numpy as jnp
from jax import lax
from jax.experimental import pallas as pl
from jax.experimental.pallas import tpu as pltpu
from jax.sharding import PartitionSpec as P

HD = 64
NEG = -1e30
PAIR = 128
MESH = pl.DeviceIdType.MESH


def normalize(rows, gain):
    values = rows.astype(jnp.float32)
    center = jnp.mean(values, axis=-1, keepdims=True)
    moved = values - center
    spread = jnp.mean(jnp.square(moved), axis=-1, keepdims=True)
    return (moved * lax.rsqrt(spread + 1e-05) * gain).astype(jnp.bfloat16)


def dot(a, b):
    return jnp.dot(a, b, preferred_element_type=jnp.float32)


class Line:
    def __init__(self, axis, count, slots, send_sems, recv_sems):
        self.axis, self.count, self.slots = axis, count, slots
        self.send_sems, self.recv_sems = send_sems, recv_sems
        self.me = lax.axis_index(axis)

    def sent(self, way, step):
        if way == 0:
            return self.me - step, (self.me >= step) & (self.me < self.count - 1)
        return self.me + step, (self.me + step < self.count) & (self.me > 0)

    def got(self, way, step):
        if way == 0:
            return self.me - 1 - step, self.me >= 1 + step
        return self.me + 1 + step, self.me + 1 + step < self.count

    def copy(self, way, step, slot):
        other = self.me + 1 if way == 0 else self.me + self.count - 1
        return pltpu.make_async_remote_copy(
            src_ref=self.slots.at[slot],
            dst_ref=self.slots.at[slot],
            send_sem=self.send_sems.at[way, step],
            recv_sem=self.recv_sems.at[way, step],
            device_id={self.axis: lax.rem(other, self.count)},
            device_id_type=MESH,
        )

    def start(self, way, step):
        slot, live = self.sent(way, step)

        @pl.when(live)
        def _():
            self.copy(way, step, slot).start()

    def wait_send(self, way, step):
        slot, live = self.sent(way, step)

        @pl.when(live)
        def _():
            self.copy(way, step, slot).wait_send()

    def wait_recv(self, way, step):
        slot, live = self.got(way, step)

        @pl.when(live)
        def _():
            self.copy(way, step, slot).wait_recv()

        return slot, live

    def finish(self):
        for way in range(2):

            @pl.loop(0, self.count - 1)
            def _(step):
                self.wait_send(way, step)


def kernel(
    n_ctx,
    n_ten,
    x_ref,
    mask_ref,
    valid_ref,
    gain1_ref,
    wq_ref,
    wk_ref,
    wv_ref,
    wo_ref,
    gain2_ref,
    wp1_ref,
    wd_ref,
    bns_ref,
    bnb_ref,
    wp2_ref,
    out_ref,
    normed,
    qm,
    kv,
    wo_all,
    wp2_all,
    att,
    acc,
    top,
    total,
    res,
    gpad,
    g32,
    act,
    act_all,
    kv_ss,
    kv_rs,
    wo_ss,
    wo_rs,
    wp_ss,
    wp_rs,
    at_ss,
    at_rs,
    halo_ss,
    halo_rs,
    act_ss,
    act_rs,
):
    ctx = lax.axis_index("context")
    ten = lax.axis_index("tensor")
    frames, width = x_ref.shape
    cols = wq_ref.shape[1]
    pairs = cols // PAIR
    share = frames // n_ten
    chunk = min(frames, 128)

    barrier = pltpu.get_barrier_semaphore()
    for shift in (1, n_ctx - 1):
        pl.semaphore_signal(
            barrier, inc=1, device_id={"context": lax.rem(ctx + shift, n_ctx)}, device_id_type=MESH
        )
    for shift in range(1, n_ten):
        pl.semaphore_signal(
            barrier, inc=1, device_id={"tensor": lax.rem(ten + shift, n_ten)}, device_id_type=MESH
        )
    kv_line = Line("context", n_ctx, kv, kv_ss, kv_rs)
    wo_line = Line("tensor", n_ten, wo_all, wo_ss, wo_rs)
    wp_line = Line("tensor", n_ten, wp2_all, wp_ss, wp_rs)
    at_line = Line("tensor", n_ten, att, at_ss, at_rs)

    wo_all[ten] = wo_ref[...]
    wp2_all[ten] = wp2_ref[...]

    @pl.loop(0, frames // chunk)
    def _(i):
        rows = pl.ds(pl.multiple_of(i * chunk, chunk), chunk)
        normed[rows, :] = normalize(x_ref[rows, :], gain1_ref[...])

    big = min(frames, 256)

    @pl.loop(0, frames // big)
    def _(i):
        rows = pl.ds(pl.multiple_of(i * big, big), big)
        low = pl.ds(pl.multiple_of(frames + i * big, big), big)
        kv[ctx, rows, :] = dot(normed[rows, :], wk_ref[...]).astype(jnp.bfloat16)
        kv[ctx, low, :] = dot(normed[rows, :], wv_ref[...]).astype(jnp.bfloat16)

    kv[ctx, 2 * frames :, :] = mask_ref[...]

    pl.semaphore_wait(barrier, 2 + n_ten - 1)
    for way in range(2):
        kv_line.start(way, 0)
    for way in range(2):
        wo_line.start(way, 0)
    for way in range(2):
        wp_line.start(way, 0)

    lane = lax.broadcasted_iota(jnp.int32, (1, PAIR), 1)
    halves = (lane < HD, lane >= HD)

    @pl.loop(0, frames // big)
    def _(i):
        rows = pl.ds(pl.multiple_of(i * big, big), big)
        query = (dot(normed[rows, :], wq_ref[...]).astype(jnp.bfloat16)) * jnp.bfloat16(
            1.0 / math.sqrt(HD)
        )
        for p in range(pairs):
            part = query[:, p * PAIR : (p + 1) * PAIR]
            for h in range(2):
                qm[2 * p + h, rows, :] = jnp.where(halves[h], part, jnp.bfloat16(0))

    top[...] = jnp.full_like(top, NEG)
    acc[...] = jnp.zeros_like(acc)

    def attend(block):
        strip = kv[block, 2 * frames :, :].astype(jnp.float32)
        bias = jnp.concatenate([strip[i : i + 1, :] for i in range(frames // cols)], axis=1)
        for p in range(pairs):
            span = slice(p * PAIR, (p + 1) * PAIR)
            keys = kv[block, :frames, span]
            vals = kv[block, frames : 2 * frames, span]
            for h in range(2):
                head = 2 * p + h
                mixed_vals = jnp.where(halves[h], vals, jnp.bfloat16(1))

                @pl.loop(0, frames // big)
                def _(i):
                    rows = pl.ds(pl.multiple_of(i * big, big), big)
                    scores = (
                        lax.dot_general(
                            qm[head, rows, :],
                            keys,
                            (((1,), (1,)), ((), ())),
                            preferred_element_type=jnp.float32,
                        )
                        + bias
                    )
                    old = top[head, rows, :1]
                    new = jnp.maximum(old, jnp.max(scores, axis=1, keepdims=True))
                    weights = jnp.exp(scores - new).astype(jnp.bfloat16)
                    acc[head, rows, :] = acc[head, rows, :] * jnp.exp(old - new) + dot(
                        weights, mixed_vals
                    )
                    top[head, rows, :] = jnp.broadcast_to(new, (big, PAIR))

    attend(ctx)

    def weight_step(step):
        for line in (wo_line, wp_line):
            for way in range(2):
                line.wait_recv(way, step)

                @pl.when(step + 1 < n_ten - 1)
                def _():
                    line.start(way, step + 1)

    @pl.loop(0, n_ctx - 1)
    def _(step):
        for way in range(2):
            kv_line.wait_recv(way, step)

            @pl.when(step + 1 < n_ctx - 1)
            def _():
                kv_line.start(way, step + 1)

        @pl.when(step < n_ten - 1)
        def _():
            weight_step(step)

        for way in range(2):
            slot, live = kv_line.got(way, step)

            @pl.when(live)
            def _():
                attend(slot)

    for step in range(n_ctx - 1, n_ten - 1):
        weight_step(step)

    @pl.loop(0, frames // big)
    def _(i):
        rows = pl.ds(pl.multiple_of(i * big, big), big)
        for p in range(pairs):
            first, second = acc[2 * p, rows, :], acc[2 * p + 1, rows, :]
            joined = jnp.where(
                halves[0], first / first[:, HD : HD + 1], second / second[:, :1]
            )
            att[ten, rows, p * PAIR : (p + 1) * PAIR] = joined.astype(jnp.bfloat16)

    for way in range(2):
        at_line.start(way, 0)

    def project(slot, first):
        @pl.loop(0, frames // big)
        def _(i):
            rows = pl.ds(pl.multiple_of(i * big, big), big)
            base = x_ref[rows, :].astype(jnp.float32) if first else total[rows, :]
            total[rows, :] = base + dot(att[slot, rows, :], wo_all[slot])

    project(ten, True)
    for step in range(n_ten - 1):
        for way in range(2):
            at_line.wait_recv(way, step)
            if step + 1 < n_ten - 1:
                at_line.start(way, step + 1)
        for way in range(2):
            slot, live = at_line.got(way, step)

            @pl.when(live)
            def _():
                project(slot, False)

    @pl.loop(0, frames // chunk)
    def _(i):
        rows = pl.ds(pl.multiple_of(i * chunk, chunk), chunk)
        rounded = total[rows, :].astype(jnp.bfloat16)
        res[rows, :] = rounded
        normed[rows, :] = normalize(rounded, gain2_ref[...])

    edge = (gpad.shape[0] - frames) // 2

    @pl.loop(0, frames // chunk)
    def _(i):
        rows = pl.ds(pl.multiple_of(i * chunk, chunk), chunk)
        spot = pl.ds(pl.multiple_of(edge + i * chunk, 16), chunk)
        value = dot(normed[rows, :], wp1_ref[0])
        gate = dot(normed[rows, :], wp1_ref[1])
        gated = jnp.where(valid_ref[rows, :] > 0, value * jax.nn.sigmoid(gate), 0.0)
        gpad[spot, :] = gated.astype(jnp.bfloat16)

    def halo(way):
        source = pl.ds(frames, edge) if way == 0 else pl.ds(edge, edge)
        target = pl.ds(0, edge) if way == 0 else pl.ds(frames + edge, edge)
        other = ctx + 1 if way == 0 else ctx + n_ctx - 1
        return pltpu.make_async_remote_copy(
            src_ref=gpad.at[source],
            dst_ref=gpad.at[target],
            send_sem=halo_ss.at[way],
            recv_sem=halo_rs.at[way],
            device_id={"context": lax.rem(other, n_ctx)},
            device_id_type=MESH,
        )

    sends = (ctx < n_ctx - 1, ctx > 0)
    gets = (ctx > 0, ctx < n_ctx - 1)
    for way in range(2):

        @pl.when(sends[way])
        def _():
            halo(way).start()

        @pl.when(jnp.logical_not(gets[way]))
        def _():
            at = 0 if way == 0 else frames + edge
            gpad[at : at + edge, :] = jnp.zeros((edge, cols), jnp.bfloat16)

    g32[edge : edge + frames, :] = gpad[edge : edge + frames, :].astype(jnp.float32)
    for way in range(2):

        @pl.when(gets[way])
        def _():
            halo(way).wait_recv()

        at = 0 if way == 0 else frames + edge
        g32[at : at + edge, :] = gpad[at : at + edge, :].astype(jnp.float32)

    taps = wd_ref.shape[0]
    half = (taps - 1) // 2
    some = min(frames, 64)

    @pl.loop(0, frames // some)
    def _(i):
        start = pl.multiple_of(i * some, some)
        window = g32[pl.ds(start, some + 2 * edge), :]
        depth = jnp.zeros((some, cols), jnp.float32)
        for tap in range(taps):
            at = edge - half + tap
            depth = depth + window[at : at + some, :] * wd_ref[tap : tap + 1, :]
        depth = depth * bns_ref[...] + bnb_ref[...]
        act[pl.ds(start, some), :] = jax.nn.silu(depth).astype(jnp.bfloat16)

    def part(peer):
        return pl.ds(pl.multiple_of(peer * share, share), share)

    def swap(shift):
        peer = lax.rem(ten + shift, n_ten)
        return pltpu.make_async_remote_copy(
            src_ref=act.at[part(peer)],
            dst_ref=act_all.at[shift],
            send_sem=act_ss.at[shift],
            recv_sem=act_rs.at[shift],
            device_id={"tensor": peer},
            device_id_type=MESH,
        )

    for shift in range(1, n_ten):
        swap(shift).start()
    mine = part(ten)
    out = res[mine, :].astype(jnp.float32)
    out = out + dot(act[mine, :], wp2_all[ten])
    for shift in range(1, n_ten):
        swap(shift).wait_recv()
        out = out + dot(act_all[shift], wp2_all[lax.rem(ten + n_ten - shift, n_ten)])
    out_ref[...] = out.astype(jnp.bfloat16)

    for line in (kv_line, wo_line, wp_line, at_line):
        line.finish()
    for way in range(2):

        @pl.when(sends[way])
        def _():
            halo(way).wait_send()

    for shift in range(1, n_ten):
        swap(shift).wait_send()


def local(
    n_ctx,
    n_ten,
    inputs,
    frame_valid,
    norm1_gain,
    w_query,
    w_key,
    w_value,
    w_out,
    norm2_gain,
    w_point1,
    w_depth,
    bn_scale,
    bn_shift,
    w_point2,
):
    frames, width = inputs.shape
    cols = w_query.shape[1]
    heads = cols // HD
    share = frames // n_ten
    strips = frames // cols
    edge = 16
    mask = jnp.where(frame_valid > 0, 0.0, NEG).astype(jnp.bfloat16).reshape(strips, cols)
    mask = jnp.pad(mask, ((0, 16 - strips), (0, 0)))
    valid = frame_valid.astype(jnp.float32)[:, None]
    bf, f32 = jnp.bfloat16, jnp.float32
    sem = pltpu.SemaphoreType.DMA
    line = [sem((2, n_ctx - 1))] * 2 + [sem((2, n_ten - 1))] * 6
    return pl.pallas_call(
        functools.partial(kernel, n_ctx, n_ten),
        out_shape=jax.ShapeDtypeStruct((share, width), bf),
        in_specs=[pl.BlockSpec(memory_space=pltpu.VMEM)] * 14,
        out_specs=pl.BlockSpec(memory_space=pltpu.VMEM),
        scratch_shapes=[
            pltpu.VMEM((frames, width), bf),
            pltpu.VMEM((heads, frames, PAIR), bf),
            pltpu.VMEM((n_ctx, 2 * frames + 16, cols), bf),
            pltpu.VMEM((n_ten, cols, width), bf),
            pltpu.VMEM((n_ten, cols, width), bf),
            pltpu.VMEM((n_ten, frames, cols), bf),
            pltpu.VMEM((heads, frames, PAIR), f32),
            pltpu.VMEM((heads, frames, PAIR), f32),
            pltpu.VMEM((frames, width), f32),
            pltpu.VMEM((frames, width), bf),
            pltpu.VMEM((frames + 2 * edge, cols), bf),
            pltpu.VMEM((frames + 2 * edge, cols), f32),
            pltpu.VMEM((frames, cols), bf),
            pltpu.VMEM((n_ten, share, cols), bf),
        ]
        + line
        + [sem((2,)), sem((2,)), sem((n_ten,)), sem((n_ten,))],
        compiler_params=pltpu.CompilerParams(
            collective_id=0, has_side_effects=True, vmem_limit_bytes=50 * 1024 * 1024
        ),
    )(
        inputs,
        mask,
        valid,
        norm1_gain[None],
        w_query,
        w_key,
        w_value,
        w_out,
        norm2_gain[None],
        w_point1,
        w_depth,
        bn_scale[None],
        bn_shift[None],
        w_point2,
    )


def solution(mesh):
    placed = (
        P(("groups", "context"), None),
        P(("groups", "context")),
        P(),
        P(None, "tensor"),
        P(None, "tensor"),
        P(None, "tensor"),
        P("tensor", None),
        P(),
        P(None, None, "tensor"),
        P(None, "tensor"),
        P("tensor"),
        P("tensor"),
        P("tensor", None),
    )
    return jax.shard_map(
        functools.partial(local, mesh.shape["context"], mesh.shape["tensor"]),
        mesh=mesh,
        in_specs=placed,
        out_specs=P(("groups", "context", "tensor"), None),
        check_vma=False,
    )
```

time: 219 us -> 77.9 us (0.36); the launches traced: 216 us -> 77.5 us
  waiting for transfers between devices: 123 us -> 0 us
  Pallas kernels: 0 us -> 70 us
  matrix products: 36.7 us -> 0 us
  other arithmetic: 21.4 us -> 0.01 us
  between operations: 13.4 us -> 0.08 us
  blocking collectives: 9.51 us -> 0 us
  starting transfers between devices: 5.44 us -> 0 us
    pallas_call x0 -> x1, Pallas kernels: none -> 70 us  [local(): pl.pallas_call(functools.partial(kernel, n_ctx, n_ten), out_shape=jax.Sha...]
    psum x1 -> x0, waiting for transfers between devices: 50.4 us -> none  [local(): lax.psum(jnp.dot(attended, w_out, preferred_element_type=jnp.float32), 't...]
    all_gather x2 -> x0, waiting for transfers between devices: 45.4 us -> none  [the longest x1 29 us: local(): val_part = lax.all_gather(vals, 'context', axis=0, tiled=True)]
    dot_general x15 -> x0, matrix products: 36.7 us -> none  [the longest x4 13.1 us: update(): jnp.einsum('hqk,khd->qhd', weights.astype(jnp.bfloat16), val_heads, prefe...]
    reduce_scatter x1 -> x0, waiting for transfers between devices: 26.5 us -> none  [local(): lax.psum_scatter(jnp.dot(activated, w_point2, preferred_element_type=jnp....]
    reduce_sum x8 -> x0, other arithmetic: 18.7 us -> none  [the longest x4 13.1 us: update(): run_sum = run_sum * factor + jnp.sum(weights, axis=-1)]
    all_gather x1 -> x0, blocking collectives: 9.51 us -> none  [local(): valid_part = lax.all_gather(frame_valid, 'context', axis=0, tiled=True)]
    unnamed x25 -> x23, local copies, waits for them, and re-layouts: 0.06 us -> 7.16 us
  transfers between devices with their start and end apart: 6 -> 0, of which waited for: 5 -> 0; matrix products, arithmetic and copies ran while one was open for 1% -> 0% of each run, Pallas kernels for 0% -> 0%
where the time goes in v1:
time: 77.9 us; the launch traced here: 77.5 us
  Pallas kernels  70 us (90%)
  local copies, waits for them, and re-layouts  7.33 us (9%)
    pallas_call x1, Pallas kernels, local(): pl.pallas_call(functools.partial(kernel, n_ctx, n_ten), out_shape=jax.Sha...  70 us
    unnamed x23, local copies, waits for them, and re-layouts  7.16 us

profile of v1, /device:TPU:11, one launch (start us, length us, event | category | flops | bytes accessed | tf_op | source)
XLA Modules:
  0.0 77.5 jit_solution(13488691094643434130)
XLA Ops:
  0.0 0.0 copy-start.10
  0.0 0.7 copy-done.10
  0.7 0.0 copy-start.5
  0.7 0.0 copy-start.6
  0.7 0.0 copy-start.7
  0.8 0.0 copy-start.8
  0.8 0.0 copy-start.9
  0.8 0.1 copy.14.valid_ref
  0.9 0.5 copy-done.5
  1.5 0.0 copy-done.6
  1.5 0.0 copy-done.7
  1.5 0.0 copy-done.8
  1.5 0.0 copy-done.9
  1.5 0.0 copy-start
  1.5 1.0 %copy-done = bf16[1024,256]{1,0:T(8,128)(2,1)S(1)} copy-done((bf16[1024,256]{1,0:T(8,128)(2,1)S(1)}, bf16[1024,256]{1,0:T(8,128)(2,1)}, u32[]{:S(2)}) %copy-start) | copy-done | bytes 524312
  2.5 0.0 copy-start.1
  2.5 1.0 %copy-done.1 = bf16[1024,256]{1,0:T(8,128)(2,1)S(1)} copy-done((bf16[1024,256]{1,0:T(8,128)(2,1)S(1)}, bf16[1024,256]{1,0:T(8,128)(2,1)}, u32[]{:S(2)}) %copy-start.1) | copy-done | bytes 524312
  3.6 0.0 copy-start.2
  3.6 1.0 %copy-done.2 = bf16[1024,256]{1,0:T(8,128)(2,1)S(1)} copy-done((bf16[1024,256]{1,0:T(8,128)(2,1)S(1)}, bf16[1024,256]{1,0:T(8,128)(2,1)}, u32[]{:S(2)}) %copy-start.2) | copy-done | bytes 524312
  4.6 0.0 copy-start.3
  4.6 1.0 %copy-done.3 = bf16[256,1024]{1,0:T(8,128)(2,1)S(1)} copy-done((bf16[256,1024]{1,0:T(8,128)(2,1)S(1)}, bf16[256,1024]{1,0:T(8,128)(2,1)}, u32[]{:S(2)}) %copy-start.3) | copy-done | bytes 524312
  5.7 0.0 copy-start.4
  5.7 1.0 %copy-done.4 = bf16[256,1024]{1,0:T(8,128)(2,1)S(1)} copy-done((bf16[256,1024]{1,0:T(8,128)(2,1)S(1)}, bf16[256,1024]{1,0:T(8,128)(2,1)}, u32[]{:S(2)}) %copy-start.4) | copy-done | bytes 524312
  6.7 70.0 %shard_map.127 = bf16[128,1024]{1,0:T(8,128)(2,1)S(1)} custom-call(bf16[512,1024]{1,0:T(8,128)(2,1)} %x_ref.1, bf16[16,256]{1,0:T(8,128)(2,1)S(1)} %pad.4.mask_ref, f32[512,1]{1,0:T(8,128)S(1)} %copy.14.valid_ref, f32[1,1024]{1,0:T(1,128)S(1)} %bitcast.5, bf16[1024,256]{1,0:T(8,128)(2,1)S(1)} %copy-done, bf16[1024,256]{1,0:T(8,128)(2,1)S(1)} %copy-done.1, ...), custom_call_target="tpu_custom_call" | custom-call | tf_op jit(solution)/shard_map/pallas_call | solution.py:430
  76.7 0.7 copy.16
  (4 shorter events, 0.0 us)
Async XLA Ops:
  0.0 0.7 copy-start.10
  0.7 0.8 copy-start.5
  0.7 0.8 copy-start.6
  0.7 0.7 copy-start.7
  0.8 0.7 copy-start.8
  0.8 0.7 copy-start.9
  1.5 1.0 %copy-start = (bf16[1024,256]{1,0:T(8,128)(2,1)S(1)}, bf16[1024,256]{1,0:T(8,128)(2,1)}, u32[]{:S(2)}) copy-start(bf16[1024,256]{1,0:T(8,128)(2,1)} %wq_ref.1) | copy-start | bytes 1572868
  2.5 1.0 %copy-start.1 = (bf16[1024,256]{1,0:T(8,128)(2,1)S(1)}, bf16[1024,256]{1,0:T(8,128)(2,1)}, u32[]{:S(2)}) copy-start(bf16[1024,256]{1,0:T(8,128)(2,1)} %wk_ref.1) | copy-start | bytes 1572868
  3.6 1.0 %copy-start.2 = (bf16[1024,256]{1,0:T(8,128)(2,1)S(1)}, bf16[1024,256]{1,0:T(8,128)(2,1)}, u32[]{:S(2)}) copy-start(bf16[1024,256]{1,0:T(8,128)(2,1)} %wv_ref.1) | copy-start | bytes 1572868
  4.6 1.0 %copy-start.3 = (bf16[256,1024]{1,0:T(8,128)(2,1)S(1)}, bf16[256,1024]{1,0:T(8,128)(2,1)}, u32[]{:S(2)}) copy-start(bf16[256,1024]{1,0:T(8,128)(2,1)} %wo_ref.1) | copy-start | bytes 1572868
  5.7 1.0 %copy-start.4 = (bf16[256,1024]{1,0:T(8,128)(2,1)S(1)}, bf16[256,1024]{1,0:T(8,128)(2,1)}, u32[]{:S(2)}) copy-start(bf16[256,1024]{1,0:T(8,128)(2,1)} %wp2_ref.1) | copy-start | bytes 1572868

commit v2 on v1

--- a/solution.py
+++ b/solution.py
@@ -27,8 +27,8 @@
 
 
 class Line:
-    def __init__(self, axis, count, slots, send_sems, recv_sems):
-        self.axis, self.count, self.slots = axis, count, slots
+    def __init__(self, axis, count, pick, send_sems, recv_sems):
+        self.axis, self.count, self.pick = axis, count, pick
         self.send_sems, self.recv_sems = send_sems, recv_sems
         self.me = lax.axis_index(axis)
 
@@ -45,8 +45,8 @@
     def copy(self, way, step, slot):
         other = self.me + 1 if way == 0 else self.me + self.count - 1
         return pltpu.make_async_remote_copy(
-            src_ref=self.slots.at[slot],
-            dst_ref=self.slots.at[slot],
+            src_ref=self.pick(slot),
+            dst_ref=self.pick(slot),
             send_sem=self.send_sems.at[way, step],
             recv_sem=self.recv_sems.at[way, step],
             device_id={self.axis: lax.rem(other, self.count)},
@@ -87,21 +87,29 @@
 def kernel(
     n_ctx,
     n_ten,
-    x_ref,
+    x_hbm,
     mask_ref,
     valid_ref,
     gain1_ref,
+    wq_hbm,
+    wk_hbm,
+    wv_hbm,
+    wo_hbm,
+    gain2_ref,
+    wp1_hbm,
+    wd_ref,
+    bns_ref,
+    bnb_ref,
+    wp2_hbm,
+    out_ref,
+    x_ref,
     wq_ref,
     wk_ref,
     wv_ref,
-    wo_ref,
-    gain2_ref,
     wp1_ref,
-    wd_ref,
-    bns_ref,
-    bnb_ref,
-    wp2_ref,
-    out_ref,
+    load,
+    blocks,
+    masks,
     normed,
     qm,
     kv,
@@ -118,6 +126,10 @@
     act_all,
     kv_ss,
     kv_rs,
+    mk_ss,
+    mk_rs,
+    bl_ss,
+    bl_rs,
     wo_ss,
     wo_rs,
     wp_ss,
@@ -146,45 +158,78 @@
         pl.semaphore_signal(
             barrier, inc=1, device_id={"tensor": lax.rem(ten + shift, n_ten)}, device_id_type=MESH
         )
-    kv_line = Line("context", n_ctx, kv, kv_ss, kv_rs)
-    wo_line = Line("tensor", n_ten, wo_all, wo_ss, wo_rs)
-    wp_line = Line("tensor", n_ten, wp2_all, wp_ss, wp_rs)
-    at_line = Line("tensor", n_ten, att, at_ss, at_rs)
-
-    wo_all[ten] = wo_ref[...]
-    wp2_all[ten] = wp2_ref[...]
-
-    @pl.loop(0, frames // chunk)
-    def _(i):
-        rows = pl.ds(pl.multiple_of(i * chunk, chunk), chunk)
-        normed[rows, :] = normalize(x_ref[rows, :], gain1_ref[...])
-
-    big = min(frames, 256)
-
-    @pl.loop(0, frames // big)
-    def _(i):
-        rows = pl.ds(pl.multiple_of(i * big, big), big)
-        low = pl.ds(pl.multiple_of(frames + i * big, big), big)
-        kv[ctx, rows, :] = dot(normed[rows, :], wk_ref[...]).astype(jnp.bfloat16)
-        kv[ctx, low, :] = dot(normed[rows, :], wv_ref[...]).astype(jnp.bfloat16)
-
-    kv[ctx, 2 * frames :, :] = mask_ref[...]
-
+    loads = [
+        pltpu.make_async_copy(source, target, load.at[i])
+        for i, (source, target) in enumerate(
+            (
+                (x_hbm, x_ref),
+                (wk_hbm, wk_ref),
+                (wv_hbm, wv_ref),
+                (wq_hbm, wq_ref),
+                (wo_hbm, wo_all.at[ten]),
+                (wp1_hbm, wp1_ref),
+                (wp2_hbm, wp2_all.at[ten]),
+            )
+        )
+    ]
+    for item in loads:
+        item.start()
+    z_line = Line("context", n_ctx, lambda slot: blocks.at[slot, ten], kv_ss, kv_rs)
+    mk_line = Line("context", n_ctx, lambda slot: masks.at[slot], mk_ss, mk_rs)
+    wo_line = Line("tensor", n_ten, lambda slot: wo_all.at[slot], wo_ss, wo_rs)
+    wp_line = Line("tensor", n_ten, lambda slot: wp2_all.at[slot], wp_ss, wp_rs)
+    at_line = Line("tensor", n_ten, lambda slot: att.at[slot], at_ss, at_rs)
+
+    def spread(block):
+        return Line(
+            "tensor",
+            n_ten,
+            lambda slot: blocks.at[block, slot],
+            bl_ss.at[block],
+            bl_rs.at[block],
+        )
+
+    masks[ctx] = mask_ref[...]
+    loads[0].wait()
+
+    def norm_part(i):
+        rows = pl.ds(pl.multiple_of(i * share, share), share)
+        blocks[ctx, i] = normalize(x_ref[rows, :], gain1_ref[...])
+
+    norm_part(ten)
     pl.semaphore_wait(barrier, 2 + n_ten - 1)
-    for way in range(2):
-        kv_line.start(way, 0)
+    for line in (mk_line, z_line):
+        for way in range(2):
+            line.start(way, 0)
+    loads[4].wait()
     for way in range(2):
         wo_line.start(way, 0)
-    for way in range(2):
-        wp_line.start(way, 0)
-
+
+    @pl.loop(1, n_ten)
+    def _(shift):
+        norm_part(lax.rem(ten + shift, n_ten))
+
+    def project_kv(block, spot):
+        @pl.loop(0, n_ten)
+        def _(i):
+            rows = pl.ds(pl.multiple_of(i * share, share), share)
+            low = pl.ds(pl.multiple_of(frames + i * share, share), share)
+            part = blocks[block, i]
+            kv[spot, rows, :] = dot(part, wk_ref[...]).astype(jnp.bfloat16)
+            kv[spot, low, :] = dot(part, wv_ref[...]).astype(jnp.bfloat16)
+
+    big = min(frames, 256)
     lane = lax.broadcasted_iota(jnp.int32, (1, PAIR), 1)
     halves = (lane < HD, lane >= HD)
 
-    @pl.loop(0, frames // big)
+    for item in loads[1:4]:
+        item.wait()
+    project_kv(ctx, 0)
+
+    @pl.loop(0, n_ten)
     def _(i):
-        rows = pl.ds(pl.multiple_of(i * big, big), big)
-        query = (dot(normed[rows, :], wq_ref[...]).astype(jnp.bfloat16)) * jnp.bfloat16(
+        rows = pl.ds(pl.multiple_of(i * share, share), share)
+        query = (dot(blocks[ctx, i], wq_ref[...]).astype(jnp.bfloat16)) * jnp.bfloat16(
             1.0 / math.sqrt(HD)
         )
         for p in range(pairs):
@@ -195,13 +240,13 @@
     top[...] = jnp.full_like(top, NEG)
     acc[...] = jnp.zeros_like(acc)
 
-    def attend(block):
-        strip = kv[block, 2 * frames :, :].astype(jnp.float32)
+    def attend(block, spot, p):
+        strip = masks[block].astype(jnp.float32)
         bias = jnp.concatenate([strip[i : i + 1, :] for i in range(frames // cols)], axis=1)
-        for p in range(pairs):
+        if True:
             span = slice(p * PAIR, (p + 1) * PAIR)
-            keys = kv[block, :frames, span]
-            vals = kv[block, frames : 2 * frames, span]
+            keys = kv[spot, :frames, span]
+            vals = kv[spot, frames : 2 * frames, span]
             for h in range(2):
                 head = 2 * p + h
                 mixed_vals = jnp.where(halves[h], vals, jnp.bfloat16(1))
@@ -226,39 +271,77 @@
                     )
                     top[head, rows, :] = jnp.broadcast_to(new, (big, PAIR))
 
-    attend(ctx)
-
-    def weight_step(step):
-        for line in (wo_line, wp_line):
-            for way in range(2):
-                line.wait_recv(way, step)
-
-                @pl.when(step + 1 < n_ten - 1)
-                def _():
-                    line.start(way, step + 1)
+    def weight_step(line, step):
+        for way in range(2):
+            line.wait_recv(way, step)
+
+            @pl.when(step + 1 < n_ten - 1)
+            def _():
+                line.start(way, step + 1)
+
+    def arrive(step):
+        for way in range(2):
+            mk_line.wait_recv(way, step)
+            slot, live = z_line.wait_recv(way, step)
+
+            @pl.when(step + 1 < n_ctx - 1)
+            def _():
+                z_line.start(way, step + 1)
+                mk_line.start(way, step + 1)
+
+            @pl.when(live)
+            def _():
+                for side in range(2):
+                    spread(slot).start(side, 0)
+
+    def relay(step, hop):
+        for way in range(2):
+            slot, live = z_line.got(way, step)
+
+            @pl.when(live)
+            def _():
+                for side in range(2):
+                    spread(slot).wait_recv(side, hop)
+                    if hop + 1 < n_ten - 1:
+                        spread(slot).start(side, hop + 1)
+
+    def work(jobs, step):
+        for p in range(pairs):
+            for block, spot, live in jobs:
+                pl.when(live)(lambda: attend(block, spot, p))
+            hops = [p] if p < pairs - 1 else range(pairs - 1, n_ten - 2)
+            for hop in hops:
+                if hop < n_ten - 2:
+
+                    @pl.when(step < n_ctx - 1)
+                    def _():
+                        relay(step, hop)
+
+    arrive(0)
+    work([(ctx, 0, ctx >= 0)], 0)
 
     @pl.loop(0, n_ctx - 1)
     def _(step):
-        for way in range(2):
-            kv_line.wait_recv(way, step)
-
-            @pl.when(step + 1 < n_ctx - 1)
-            def _():
-                kv_line.start(way, step + 1)
+        @pl.when(step + 1 < n_ctx - 1)
+        def _():
+            arrive(step + 1)
 
         @pl.when(step < n_ten - 1)
         def _():
-            weight_step(step)
-
-        for way in range(2):
-            slot, live = kv_line.got(way, step)
-
-            @pl.when(live)
-            def _():
-                attend(slot)
+            weight_step(wo_line, step)
+
+        relay(step, n_ten - 2)
+        jobs = []
+        for way in range(2):
+            slot, live = z_line.got(way, step)
+            pl.when(live)(lambda: project_kv(slot, way))
+            jobs.append((slot, way, live))
+        work(jobs, step + 1)
 
     for step in range(n_ctx - 1, n_ten - 1):
-        weight_step(step)
+        weight_step(wo_line, step)
+    loads[5].wait()
+    loads[6].wait()
 
     @pl.loop(0, frames // big)
     def _(i):
@@ -280,6 +363,8 @@
             base = x_ref[rows, :].astype(jnp.float32) if first else total[rows, :]
             total[rows, :] = base + dot(att[slot, rows, :], wo_all[slot])
 
+    for way in range(2):
+        wp_line.start(way, 0)
     project(ten, True)
     for step in range(n_ten - 1):
         for way in range(2):
@@ -300,6 +385,7 @@
         res[rows, :] = rounded
         normed[rows, :] = normalize(rounded, gain2_ref[...])
 
+    weight_step(wp_line, 0)
     edge = (gpad.shape[0] - frames) // 2
 
     @pl.loop(0, frames // chunk)
@@ -337,6 +423,8 @@
             at = 0 if way == 0 else frames + edge
             gpad[at : at + edge, :] = jnp.zeros((edge, cols), jnp.bfloat16)
 
+    if n_ten > 2:
+        weight_step(wp_line, 1)
     g32[edge : edge + frames, :] = gpad[edge : edge + frames, :].astype(jnp.float32)
     for way in range(2):
 
@@ -378,6 +466,8 @@
 
     for shift in range(1, n_ten):
         swap(shift).start()
+    for step in range(2, n_ten - 1):
+        weight_step(wp_line, step)
     mine = part(ten)
     out = res[mine, :].astype(jnp.float32)
     out = out + dot(act[mine, :], wp2_all[ten])
@@ -386,8 +476,15 @@
         out = out + dot(act_all[shift], wp2_all[lax.rem(ten + n_ten - shift, n_ten)])
     out_ref[...] = out.astype(jnp.bfloat16)
 
-    for line in (kv_line, wo_line, wp_line, at_line):
+    for line in (z_line, mk_line, wo_line, wp_line, at_line):
         line.finish()
+
+    @pl.loop(0, n_ctx)
+    def _(block):
+        @pl.when(block != ctx)
+        def _():
+            spread(block).finish()
+
     for way in range(2):
 
         @pl.when(sends[way])
@@ -426,16 +523,24 @@
     valid = frame_valid.astype(jnp.float32)[:, None]
     bf, f32 = jnp.bfloat16, jnp.float32
     sem = pltpu.SemaphoreType.DMA
-    line = [sem((2, n_ctx - 1))] * 2 + [sem((2, n_ten - 1))] * 6
+    line = [sem((2, n_ctx - 1))] * 4 + [sem((n_ctx, 2, n_ten - 1))] * 2 + [sem((2, n_ten - 1))] * 6
     return pl.pallas_call(
         functools.partial(kernel, n_ctx, n_ten),
         out_shape=jax.ShapeDtypeStruct((share, width), bf),
-        in_specs=[pl.BlockSpec(memory_space=pltpu.VMEM)] * 14,
+        in_specs=[pl.BlockSpec(memory_space=pl.ANY if i in (0, 4, 5, 6, 7, 9, 13) else pltpu.VMEM) for i in range(14)],
         out_specs=pl.BlockSpec(memory_space=pltpu.VMEM),
         scratch_shapes=[
             pltpu.VMEM((frames, width), bf),
+            pltpu.VMEM((width, cols), bf),
+            pltpu.VMEM((width, cols), bf),
+            pltpu.VMEM((width, cols), bf),
+            pltpu.VMEM((2, width, cols), bf),
+            sem((7,)),
+            pltpu.VMEM((n_ctx, n_ten, share, width), bf),
+            pltpu.VMEM((n_ctx, 16, cols), bf),
+            pltpu.VMEM((frames, width), bf),
             pltpu.VMEM((heads, frames, PAIR), bf),
-            pltpu.VMEM((n_ctx, 2 * frames + 16, cols), bf),
+            pltpu.VMEM((2, 2 * frames, cols), bf),
             pltpu.VMEM((n_ten, cols, width), bf),
             pltpu.VMEM((n_ten, cols, width), bf),
             pltpu.VMEM((n_ten, frames, cols), bf),
@@ -451,7 +556,7 @@
         + line
         + [sem((2,)), sem((2,)), sem((n_ten,)), sem((n_ten,))],
         compiler_params=pltpu.CompilerParams(
-            collective_id=0, has_side_effects=True, vmem_limit_bytes=50 * 1024 * 1024
+            collective_id=0, has_side_effects=True, vmem_limit_bytes=60 * 1024 * 1024
         ),
     )(
         inputs,

time: 77.9 us -> 84.7 us (1.087)
  the two profiles are of different devices: /device:TPU:11 before, /device:TPU:3 now
where the time goes in v2:
time: 84.7 us; the launch traced here: 84.5 us
  Pallas kernels  80.6 us (95%)
  local copies, waits for them, and re-layouts  3.83 us (5%)
    pallas_call x1, Pallas kernels, local(): pl.pallas_call(functools.partial(kernel, n_ctx, n_ten), out_shape=jax.Sha...  80.6 us
    unnamed x3, local copies, waits for them, and re-layouts  2.35 us

profile of v2, /device:TPU:3, one launch (start us, length us, event | category | flops | bytes accessed | tf_op | source)
XLA Modules:
  0.0 84.5 jit_solution(247880509482202418)
XLA Ops:
  0.0 0.0 copy-start
  0.0 0.7 copy-done
  0.7 0.6 pad.4.mask_ref
  1.3 0.9 %copy.14.valid_ref = f32[512,1]{1,0:T(8,128)} copy(f32[512,1]{0,1:T(1,128)S(1)} %bitcast.5) | data formatting | bytes 4096 | tf_op jit(solution)/shard_map/broadcast_in_dim | solution.py:523
  2.2 80.6 %shard_map.127 = bf16[128,1024]{1,0:T(8,128)(2,1)} custom-call(bf16[512,1024]{1,0:T(8,128)(2,1)} %x_hbm.1, bf16[16,256]{1,0:T(8,128)(2,1)} %pad.4.mask_ref, f32[512,1]{1,0:T(8,128)} %copy.14.valid_ref, f32[1,1024]{1,0:T(1,128)} %bitcast.6, bf16[1024,256]{1,0:T(8,128)(2,1)} %wq_hbm.1, bf16[1024,256]{1,0:T(8,128)(2,1)} %wk_hbm.1, bf16[1024,256]{1,0:T(8,128)(2,1)} %wv_hbm.1, ...), custom_call_target="tpu_custom_call" | custom-call | tf_op jit(solution)/shard_map/pallas_call | solution.py:527
  82.8 1.7 %copy.16 = bf16[128,1024]{1,0:T(8,128)(2,1)} copy(bf16[128,1024]{1,0:T(8,128)(2,1)} %shard_map.127) | data formatting | bytes 524288
  (3 shorter events, 0.0 us)
Async XLA Ops:
  0.0 0.7 copy-start

commit v3 on v1

--- a/solution.py
+++ b/solution.py
@@ -27,8 +27,8 @@
 
 
 class Line:
-    def __init__(self, axis, count, slots, send_sems, recv_sems):
-        self.axis, self.count, self.slots = axis, count, slots
+    def __init__(self, axis, count, pick, send_sems, recv_sems):
+        self.axis, self.count, self.pick = axis, count, pick
         self.send_sems, self.recv_sems = send_sems, recv_sems
         self.me = lax.axis_index(axis)
 
@@ -45,8 +45,8 @@
     def copy(self, way, step, slot):
         other = self.me + 1 if way == 0 else self.me + self.count - 1
         return pltpu.make_async_remote_copy(
-            src_ref=self.slots.at[slot],
-            dst_ref=self.slots.at[slot],
+            src_ref=self.pick(slot),
+            dst_ref=self.pick(slot),
             send_sem=self.send_sems.at[way, step],
             recv_sem=self.recv_sems.at[way, step],
             device_id={self.axis: lax.rem(other, self.count)},
@@ -87,21 +87,28 @@
 def kernel(
     n_ctx,
     n_ten,
-    x_ref,
+    x_hbm,
     mask_ref,
     valid_ref,
     gain1_ref,
+    wq_hbm,
+    wk_hbm,
+    wv_hbm,
+    wo_hbm,
+    gain2_ref,
+    wp1_hbm,
+    wd_ref,
+    bns_ref,
+    bnb_ref,
+    wp2_hbm,
+    out_ref,
+    x_ref,
     wq_ref,
     wk_ref,
     wv_ref,
-    wo_ref,
-    gain2_ref,
     wp1_ref,
-    wd_ref,
-    bns_ref,
-    bnb_ref,
-    wp2_ref,
-    out_ref,
+    load,
+    masks,
     normed,
     qm,
     kv,
@@ -118,6 +125,8 @@
     act_all,
     kv_ss,
     kv_rs,
+    mk_ss,
+    mk_rs,
     wo_ss,
     wo_rs,
     wp_ss,
@@ -146,13 +155,33 @@
         pl.semaphore_signal(
             barrier, inc=1, device_id={"tensor": lax.rem(ten + shift, n_ten)}, device_id_type=MESH
         )
-    kv_line = Line("context", n_ctx, kv, kv_ss, kv_rs)
-    wo_line = Line("tensor", n_ten, wo_all, wo_ss, wo_rs)
-    wp_line = Line("tensor", n_ten, wp2_all, wp_ss, wp_rs)
-    at_line = Line("tensor", n_ten, att, at_ss, at_rs)
-
-    wo_all[ten] = wo_ref[...]
-    wp2_all[ten] = wp2_ref[...]
+    loads = [
+        pltpu.make_async_copy(source, target, load.at[i])
+        for i, (source, target) in enumerate(
+            (
+                (x_hbm, x_ref),
+                (wk_hbm, wk_ref),
+                (wv_hbm, wv_ref),
+                (wq_hbm, wq_ref),
+                (wo_hbm, wo_all.at[ten]),
+                (wp1_hbm, wp1_ref),
+                (wp2_hbm, wp2_all.at[ten]),
+            )
+        )
+    ]
+    for item in loads:
+        item.start()
+
+    def pair_line(axis, count, slots, p, send_sems, recv_sems):
+        return Line(axis, count, lambda slot: slots.at[slot, p], send_sems.at[p], recv_sems.at[p])
+
+    kv_lines = [pair_line("context", n_ctx, kv, p, kv_ss, kv_rs) for p in range(pairs)]
+    at_lines = [pair_line("tensor", n_ten, att, p, at_ss, at_rs) for p in range(pairs)]
+    mk_line = Line("context", n_ctx, lambda slot: masks.at[slot], mk_ss, mk_rs)
+    wo_line = Line("tensor", n_ten, lambda slot: wo_all.at[slot], wo_ss, wo_rs)
+    wp_line = Line("tensor", n_ten, lambda slot: wp2_all.at[slot], wp_ss, wp_rs)
+    masks[ctx] = mask_ref[...]
+    loads[0].wait()
 
     @pl.loop(0, frames // chunk)
     def _(i):
@@ -160,23 +189,29 @@
         normed[rows, :] = normalize(x_ref[rows, :], gain1_ref[...])
 
     big = min(frames, 256)
+    loads[1].wait()
+    loads[2].wait()
 
     @pl.loop(0, frames // big)
     def _(i):
         rows = pl.ds(pl.multiple_of(i * big, big), big)
         low = pl.ds(pl.multiple_of(frames + i * big, big), big)
-        kv[ctx, rows, :] = dot(normed[rows, :], wk_ref[...]).astype(jnp.bfloat16)
-        kv[ctx, low, :] = dot(normed[rows, :], wv_ref[...]).astype(jnp.bfloat16)
-
-    kv[ctx, 2 * frames :, :] = mask_ref[...]
+        keys = dot(normed[rows, :], wk_ref[...]).astype(jnp.bfloat16)
+        vals = dot(normed[rows, :], wv_ref[...]).astype(jnp.bfloat16)
+        for p in range(pairs):
+            kv[ctx, p, rows, :] = keys[:, p * PAIR : (p + 1) * PAIR]
+            kv[ctx, p, low, :] = vals[:, p * PAIR : (p + 1) * PAIR]
 
     pl.semaphore_wait(barrier, 2 + n_ten - 1)
-    for way in range(2):
-        kv_line.start(way, 0)
-    for way in range(2):
-        wo_line.start(way, 0)
-    for way in range(2):
-        wp_line.start(way, 0)
+    for line in [mk_line] + kv_lines:
+        for way in range(2):
+            line.start(way, 0)
+    loads[4].wait()
+    loads[6].wait()
+    for line in (wo_line, wp_line):
+        for way in range(2):
+            line.start(way, 0)
+    loads[3].wait()
 
     lane = lax.broadcasted_iota(jnp.int32, (1, PAIR), 1)
     halves = (lane < HD, lane >= HD)
@@ -195,13 +230,12 @@
     top[...] = jnp.full_like(top, NEG)
     acc[...] = jnp.zeros_like(acc)
 
-    def attend(block):
-        strip = kv[block, 2 * frames :, :].astype(jnp.float32)
+    def attend(block, p):
+        strip = masks[block].astype(jnp.float32)
         bias = jnp.concatenate([strip[i : i + 1, :] for i in range(frames // cols)], axis=1)
-        for p in range(pairs):
-            span = slice(p * PAIR, (p + 1) * PAIR)
-            keys = kv[block, :frames, span]
-            vals = kv[block, frames : 2 * frames, span]
+        if True:
+            keys = kv[block, p, :frames, :]
+            vals = kv[block, p, frames:, :]
             for h in range(2):
                 head = 2 * p + h
                 mixed_vals = jnp.where(halves[h], vals, jnp.bfloat16(1))
@@ -226,7 +260,8 @@
                     )
                     top[head, rows, :] = jnp.broadcast_to(new, (big, PAIR))
 
-    attend(ctx)
+    for p in range(pairs):
+        attend(ctx, p)
 
     def weight_step(step):
         for line in (wo_line, wp_line):
@@ -237,57 +272,61 @@
                 def _():
                     line.start(way, step + 1)
 
-    @pl.loop(0, n_ctx - 1)
+    def close(p):
+        @pl.loop(0, frames // big)
+        def _(i):
+            rows = pl.ds(pl.multiple_of(i * big, big), big)
+            first, second = acc[2 * p, rows, :], acc[2 * p + 1, rows, :]
+            joined = jnp.where(halves[0], first / first[:, HD : HD + 1], second / second[:, :1])
+            att[ten, p, rows, :] = joined.astype(jnp.bfloat16)
+
+        for way in range(2):
+            at_lines[p].start(way, 0)
+
+    def visit(step, last):
+        @pl.when(step < n_ten - 1)
+        def _():
+            weight_step(step)
+
+        for p in range(pairs):
+            for line in ([mk_line] if p == 0 else []) + [kv_lines[p]]:
+                for way in range(2):
+                    line.wait_recv(way, step)
+                    if not last:
+                        line.start(way, step + 1)
+            for way in range(2):
+                slot, live = kv_lines[p].got(way, step)
+                pl.when(live)(lambda: attend(slot, p))
+            if last:
+                close(p)
+
+    @pl.loop(0, n_ctx - 2)
     def _(step):
-        for way in range(2):
-            kv_line.wait_recv(way, step)
-
-            @pl.when(step + 1 < n_ctx - 1)
-            def _():
-                kv_line.start(way, step + 1)
-
-        @pl.when(step < n_ten - 1)
-        def _():
-            weight_step(step)
-
-        for way in range(2):
-            slot, live = kv_line.got(way, step)
-
-            @pl.when(live)
-            def _():
-                attend(slot)
-
+        visit(step, False)
+
+    visit(n_ctx - 2, True)
     for step in range(n_ctx - 1, n_ten - 1):
         weight_step(step)
-
-    @pl.loop(0, frames // big)
-    def _(i):
-        rows = pl.ds(pl.multiple_of(i * big, big), big)
-        for p in range(pairs):
-            first, second = acc[2 * p, rows, :], acc[2 * p + 1, rows, :]
-            joined = jnp.where(
-                halves[0], first / first[:, HD : HD + 1], second / second[:, :1]
-            )
-            att[ten, rows, p * PAIR : (p + 1) * PAIR] = joined.astype(jnp.bfloat16)
-
-    for way in range(2):
-        at_line.start(way, 0)
 
     def project(slot, first):
         @pl.loop(0, frames // big)
         def _(i):
             rows = pl.ds(pl.multiple_of(i * big, big), big)
             base = x_ref[rows, :].astype(jnp.float32) if first else total[rows, :]
-            total[rows, :] = base + dot(att[slot, rows, :], wo_all[slot])
+            total[rows, :] = base + dot(
+                jnp.concatenate([att[slot, p, rows, :] for p in range(pairs)], axis=1),
+                wo_all[slot],
+            )
 
     project(ten, True)
     for step in range(n_ten - 1):
         for way in range(2):
-            at_line.wait_recv(way, step)
-            if step + 1 < n_ten - 1:
-                at_line.start(way, step + 1)
+            for line in at_lines:
+                line.wait_recv(way, step)
+                if step + 1 < n_ten - 1:
+                    line.start(way, step + 1)
         for way in range(2):
-            slot, live = at_line.got(way, step)
+            slot, live = at_lines[0].got(way, step)
 
             @pl.when(live)
             def _():
@@ -300,6 +339,7 @@
         res[rows, :] = rounded
         normed[rows, :] = normalize(rounded, gain2_ref[...])
 
+    loads[5].wait()
     edge = (gpad.shape[0] - frames) // 2
 
     @pl.loop(0, frames // chunk)
@@ -386,7 +426,7 @@
         out = out + dot(act_all[shift], wp2_all[lax.rem(ten + n_ten - shift, n_ten)])
     out_ref[...] = out.astype(jnp.bfloat16)
 
-    for line in (kv_line, wo_line, wp_line, at_line):
+    for line in kv_lines + at_lines + [mk_line, wo_line, wp_line]:
         line.finish()
     for way in range(2):
 
@@ -426,19 +466,31 @@
     valid = frame_valid.astype(jnp.float32)[:, None]
     bf, f32 = jnp.bfloat16, jnp.float32
     sem = pltpu.SemaphoreType.DMA
-    line = [sem((2, n_ctx - 1))] * 2 + [sem((2, n_ten - 1))] * 6
+    line = (
+        [sem((cols // PAIR, 2, n_ctx - 1))] * 2
+        + [sem((2, n_ctx - 1))] * 2
+        + [sem((2, n_ten - 1))] * 4
+        + [sem((cols // PAIR, 2, n_ten - 1))] * 2
+    )
     return pl.pallas_call(
         functools.partial(kernel, n_ctx, n_ten),
         out_shape=jax.ShapeDtypeStruct((share, width), bf),
-        in_specs=[pl.BlockSpec(memory_space=pltpu.VMEM)] * 14,
+        in_specs=[pl.BlockSpec(memory_space=pl.ANY if i in (0, 4, 5, 6, 7, 9, 13) else pltpu.VMEM) for i in range(14)],
         out_specs=pl.BlockSpec(memory_space=pltpu.VMEM),
         scratch_shapes=[
             pltpu.VMEM((frames, width), bf),
+            pltpu.VMEM((width, cols), bf),
+            pltpu.VMEM((width, cols), bf),
+            pltpu.VMEM((width, cols), bf),
+            pltpu.VMEM((2, width, cols), bf),
+            sem((7,)),
+            pltpu.VMEM((n_ctx, 16, cols), bf),
+            pltpu.VMEM((frames, width), bf),
             pltpu.VMEM((heads, frames, PAIR), bf),
-            pltpu.VMEM((n_ctx, 2 * frames + 16, cols), bf),
+            pltpu.VMEM((n_ctx, cols // PAIR, 2 * frames, PAIR), bf),
             pltpu.VMEM((n_ten, cols, width), bf),
             pltpu.VMEM((n_ten, cols, width), bf),
-            pltpu.VMEM((n_ten, frames, cols), bf),
+            pltpu.VMEM((n_ten, cols // PAIR, frames, PAIR), bf),
             pltpu.VMEM((heads, frames, PAIR), f32),
             pltpu.VMEM((heads, frames, PAIR), f32),
             pltpu.VMEM((frames, width), f32),
@@ -451,7 +503,7 @@
         + line
         + [sem((2,)), sem((2,)), sem((n_ten,)), sem((n_ten,))],
         compiler_params=pltpu.CompilerParams(
-            collective_id=0, has_side_effects=True, vmem_limit_bytes=50 * 1024 * 1024
+            collective_id=0, has_side_effects=True, vmem_limit_bytes=60 * 1024 * 1024
         ),
     )(
         inputs,

time: 77.9 us -> 70.4 us (0.904)
  Pallas kernels: 70 us -> 66.4 us
  local copies, waits for them, and re-layouts: 7.33 us -> 3.83 us
    unnamed x23 -> x3, local copies, waits for them, and re-layouts: 7.16 us -> 2.35 us
    pallas_call x1, Pallas kernels: 70 us -> 66.4 us  [local(): pl.pallas_call(functools.partial(kernel, n_ctx, n_ten), out_shape=jax.Sha...]
where the time goes in v3:
time: 70.4 us; the launch traced here: 70.3 us
  Pallas kernels  66.4 us (94%)
  local copies, waits for them, and re-layouts  3.83 us (5%)
    pallas_call x1, Pallas kernels, local(): pl.pallas_call(functools.partial(kernel, n_ctx, n_ten), out_shape=jax.Sha...  66.4 us
    unnamed x3, local copies, waits for them, and re-layouts  2.35 us

profile of v3, /device:TPU:11, one launch (start us, length us, event | category | flops | bytes accessed | tf_op | source)
XLA Modules:
  0.0 70.3 jit_solution(13154381386466053665)
XLA Ops:
  0.0 0.0 copy-start
  0.0 0.7 copy-done
  0.7 0.6 pad.4.mask_ref
  1.3 0.9 %copy.14.valid_ref = f32[512,1]{1,0:T(8,128)} copy(f32[512,1]{0,1:T(1,128)S(1)} %bitcast.5) | data formatting | bytes 4096 | tf_op jit(solution)/shard_map/broadcast_in_dim | solution.py:466
  2.2 66.4 %shard_map.127 = bf16[128,1024]{1,0:T(8,128)(2,1)} custom-call(bf16[512,1024]{1,0:T(8,128)(2,1)} %x_hbm.1, bf16[16,256]{1,0:T(8,128)(2,1)} %pad.4.mask_ref, f32[512,1]{1,0:T(8,128)} %copy.14.valid_ref, f32[1,1024]{1,0:T(1,128)} %bitcast.6, bf16[1024,256]{1,0:T(8,128)(2,1)} %wq_hbm.1, bf16[1024,256]{1,0:T(8,128)(2,1)} %wk_hbm.1, bf16[1024,256]{1,0:T(8,128)(2,1)} %wv_hbm.1, ...), custom_call_target="tpu_custom_call" | custom-call | tf_op jit(solution)/shard_map/pallas_call | solution.py:475
  68.6 1.7 %copy.16 = bf16[128,1024]{1,0:T(8,128)(2,1)} copy(bf16[128,1024]{1,0:T(8,128)(2,1)} %shard_map.127) | data formatting | bytes 524288
  (3 shorter events, 0.0 us)
Async XLA Ops:
  0.0 0.7 copy-start

commit v4 on v3

--- a/solution.py
+++ b/solution.py
@@ -183,21 +183,18 @@
     masks[ctx] = mask_ref[...]
     loads[0].wait()
 
-    @pl.loop(0, frames // chunk)
-    def _(i):
-        rows = pl.ds(pl.multiple_of(i * chunk, chunk), chunk)
-        normed[rows, :] = normalize(x_ref[rows, :], gain1_ref[...])
-
     big = min(frames, 256)
     loads[1].wait()
     loads[2].wait()
 
-    @pl.loop(0, frames // big)
+    @pl.loop(0, frames // chunk, unroll=True)
     def _(i):
-        rows = pl.ds(pl.multiple_of(i * big, big), big)
-        low = pl.ds(pl.multiple_of(frames + i * big, big), big)
-        keys = dot(normed[rows, :], wk_ref[...]).astype(jnp.bfloat16)
-        vals = dot(normed[rows, :], wv_ref[...]).astype(jnp.bfloat16)
+        rows = pl.ds(pl.multiple_of(i * chunk, chunk), chunk)
+        low = pl.ds(pl.multiple_of(frames + i * chunk, chunk), chunk)
+        part = normalize(x_ref[rows, :], gain1_ref[...])
+        normed[rows, :] = part
+        keys = dot(part, wk_ref[...]).astype(jnp.bfloat16)
+        vals = dot(part, wv_ref[...]).astype(jnp.bfloat16)
         for p in range(pairs):
             kv[ctx, p, rows, :] = keys[:, p * PAIR : (p + 1) * PAIR]
             kv[ctx, p, low, :] = vals[:, p * PAIR : (p + 1) * PAIR]
@@ -216,7 +213,7 @@
     lane = lax.broadcasted_iota(jnp.int32, (1, PAIR), 1)
     halves = (lane < HD, lane >= HD)
 
-    @pl.loop(0, frames // big)
+    @pl.loop(0, frames // big, unroll=True)
     def _(i):
         rows = pl.ds(pl.multiple_of(i * big, big), big)
         query = (dot(normed[rows, :], wq_ref[...]).astype(jnp.bfloat16)) * jnp.bfloat16(
@@ -240,7 +237,7 @@
                 head = 2 * p + h
                 mixed_vals = jnp.where(halves[h], vals, jnp.bfloat16(1))
 
-                @pl.loop(0, frames // big)
+                @pl.loop(0, frames // big, unroll=True)
                 def _(i):
                     rows = pl.ds(pl.multiple_of(i * big, big), big)
                     scores = (
@@ -273,7 +270,7 @@
                     line.start(way, step + 1)
 
     def close(p):
-        @pl.loop(0, frames // big)
+        @pl.loop(0, frames // big, unroll=True)
         def _(i):
             rows = pl.ds(pl.multiple_of(i * big, big), big)
             first, second = acc[2 * p, rows, :], acc[2 * p + 1, rows, :]
@@ -309,7 +306,7 @@
         weight_step(step)
 
     def project(slot, first):
-        @pl.loop(0, frames // big)
+        @pl.loop(0, frames // big, unroll=True)
         def _(i):
             rows = pl.ds(pl.multiple_of(i * big, big), big)
             base = x_ref[rows, :].astype(jnp.float32) if first else total[rows, :]
@@ -332,22 +329,18 @@
             def _():
                 project(slot, False)
 
-    @pl.loop(0, frames // chunk)
-    def _(i):
-        rows = pl.ds(pl.multiple_of(i * chunk, chunk), chunk)
-        rounded = total[rows, :].astype(jnp.bfloat16)
-        res[rows, :] = rounded
-        normed[rows, :] = normalize(rounded, gain2_ref[...])
-
     loads[5].wait()
     edge = (gpad.shape[0] - frames) // 2
 
-    @pl.loop(0, frames // chunk)
+    @pl.loop(0, frames // chunk, unroll=True)
     def _(i):
         rows = pl.ds(pl.multiple_of(i * chunk, chunk), chunk)
         spot = pl.ds(pl.multiple_of(edge + i * chunk, 16), chunk)
-        value = dot(normed[rows, :], wp1_ref[0])
-        gate = dot(normed[rows, :], wp1_ref[1])
+        rounded = total[rows, :].astype(jnp.bfloat16)
+        res[rows, :] = rounded
+        part = normalize(rounded, gain2_ref[...])
+        value = dot(part, wp1_ref[0])
+        gate = dot(part, wp1_ref[1])
         gated = jnp.where(valid_ref[rows, :] > 0, value * jax.nn.sigmoid(gate), 0.0)
         gpad[spot, :] = gated.astype(jnp.bfloat16)
 

time: 70.4 us -> 67.9 us (0.964)
  Pallas kernels: 66.4 us -> 63.8 us
    pallas_call x1, Pallas kernels: 66.4 us -> 63.8 us  [local(): pl.pallas_call(functools.partial(kernel, n_ctx, n_ten), out_shape=jax.Sha...]
where the time goes in v4:
time: 67.9 us; the launch traced here: 67.7 us
  Pallas kernels  63.8 us (94%)
  local copies, waits for them, and re-layouts  3.83 us (6%)
    pallas_call x1, Pallas kernels, local(): pl.pallas_call(functools.partial(kernel, n_ctx, n_ten), out_shape=jax.Sha...  63.8 us
    unnamed x3, local copies, waits for them, and re-layouts  2.35 us

profile of v4, /device:TPU:11, one launch (start us, length us, event | category | flops | bytes accessed | tf_op | source)
XLA Modules:
  0.0 67.7 jit_solution(5417531972160035807)
XLA Ops:
  0.0 0.0 copy-start
  0.0 0.7 %copy-done = s32[512]{0:T(512)S(1)} copy-done((s32[512]{0:T(512)S(1)}, s32[512]{0:T(512)}, u32[]{:S(2)}) %copy-start) | copy-done | bytes 2072
  0.7 0.6 pad.4.mask_ref
  1.3 0.9 %copy.14.valid_ref = f32[512,1]{1,0:T(8,128)} copy(f32[512,1]{0,1:T(1,128)S(1)} %bitcast.5) | data formatting | bytes 4096 | tf_op jit(solution)/shard_map/broadcast_in_dim | solution.py:459
  2.2 63.8 %shard_map.127 = bf16[128,1024]{1,0:T(8,128)(2,1)} custom-call(bf16[512,1024]{1,0:T(8,128)(2,1)} %x_hbm.1, bf16[16,256]{1,0:T(8,128)(2,1)} %pad.4.mask_ref, f32[512,1]{1,0:T(8,128)} %copy.14.valid_ref, f32[1,1024]{1,0:T(1,128)} %bitcast.6, bf16[1024,256]{1,0:T(8,128)(2,1)} %wq_hbm.1, bf16[1024,256]{1,0:T(8,128)(2,1)} %wk_hbm.1, bf16[1024,256]{1,0:T(8,128)(2,1)} %wv_hbm.1, ...), custom_call_target="tpu_custom_call" | custom-call | tf_op jit(solution)/shard_map/pallas_call | solution.py:468
  66.0 1.7 %copy.16 = bf16[128,1024]{1,0:T(8,128)(2,1)} copy(bf16[128,1024]{1,0:T(8,128)(2,1)} %shard_map.127) | data formatting | bytes 524288
  (3 shorter events, 0.0 us)
Async XLA Ops:
  0.0 0.7 %copy-start = (s32[512]{0:T(512)S(1)}, s32[512]{0:T(512)}, u32[]{:S(2)}) copy-start(s32[512]{0:T(512)} %param.14) | copy-start | bytes 6148
